TPU v7x, 32 devices: a whole 2x2x4 slice. The times are simulated.
32 devices in a mesh: dp: 8 (over y, x, core), tensor: 4 (over z).
Axes of the slice: x: 2, y: 2, z: 4, core: 2. Of those that a mesh axis runs over, the one named last changes fastest.
Arguments:
- out_grad: bfloat16 [8, 256, 4096], P('dp', 'tensor'), may hold values from -6 to 6
- out_weight: bfloat16 [4096, 1024], P('dp', 'tensor'), may hold values from -0.1875 to 0.1875
- queries: bfloat16 [8, 256, 1024], P('dp', None, 'tensor'), may hold values from -5 to 5
- keys: bfloat16 [8, 256, 512], P('dp', None, 'tensor'), may hold values from -5 to 5, as said below
- values: bfloat16 [8, 256, 512], P('dp', None, 'tensor'), may hold values from -6 to 6, as said below
- segment_ids: int32 [8, 256], P('dp'), may hold values from 0 to 3, never falling along the last dimension, each value on 1 to 128 neighbouring positions
Outputs:
- d_queries: bfloat16 [8, 256, 1024], P('dp', None, 'tensor')
- d_keys: bfloat16 [8, 256, 512], P('dp', None, 'tensor')
- d_values: bfloat16 [8, 256, 512], P('dp', None, 'tensor')
- d_out_weight: float32 [4096, 1024], P('dp', 'tensor')
Inputs may be any that keep to these rules, and one draw needn't show every extreme that they name: `keys`: column blocks 2 g and 2 g + 1 are equal. `values`: column blocks 2 g and 2 g + 1 are equal.
All inputs are finite; a program needn't handle non-finite values.
Results may differ from a plain program's by a relative error of at most 0.018.
Values may be sent and summed in bfloat16 or wider, within the bound.
A program may use at most 128 MiB of HBM per device.

v0:
```python
import jax
import jax.numpy as jnp
from jax import lax
from jax.sharding import PartitionSpec as P

HD = 128


def from_partner(block, axis, bit):
    count = lax.axis_size(axis)
    route = []
    for low in range(count):
        high = low | 1 << bit
        if high != low and high < count:
            route += [(low, high), (high, low)]
    return lax.ppermute(block, axis, route)


def local(out_grad, out_weight, queries, keys, values, segment_ids):
    scale = HD ** (-0.5)
    grad_local = out_grad[0]
    query_rows = queries[0]
    length = query_rows.shape[0]
    width = query_rows.shape[1]
    heads_here = width // HD
    key_local = keys[0]
    value_local = values[0]
    query_heads = query_rows.reshape(length, heads_here, HD)
    scores = (
        jnp.einsum("qhd,kd->hqk", query_heads, key_local, preferred_element_type=jnp.float32)
        * scale
    )
    segments = segment_ids[0]
    position = jnp.arange(length)
    visible = (segments[:, None] == segments[None, :]) & (position[:, None] >= position[None, :])
    masked = jnp.where(visible[None], scores, -jnp.inf)
    top_score = jnp.max(masked, axis=-1, keepdims=True)
    raw_exp = jnp.exp(masked - top_score)
    attn_prob = raw_exp / jnp.sum(raw_exp, axis=-1, keepdims=True)
    prob_low = attn_prob.astype(jnp.bfloat16)
    attn_out = jnp.einsum(
        "hqk,kd->qhd", prob_low, value_local, preferred_element_type=jnp.float32
    ).astype(jnp.bfloat16)
    flat_out = attn_out.reshape(length, width)
    grad_full = lax.all_gather(grad_local, "tensor", axis=0, tiled=True)
    columns = grad_full
    grad_sum = jnp.dot(
        columns,
        lax.all_gather(out_weight, "dp", axis=0, tiled=True),
        preferred_element_type=jnp.float32,
    )
    columns = grad_full
    weight_rows = lax.psum_scatter(
        lax.dot_general(
            columns, flat_out, (((0,), (0,)), ((), ())), preferred_element_type=jnp.float32
        ).astype(jnp.bfloat16),
        "dp",
        scatter_dimension=0,
        tiled=True,
    ).astype(jnp.float32)
    grad_attn = grad_sum.astype(jnp.bfloat16)
    grad_heads = grad_attn.reshape(length, heads_here, HD)
    deltas = jnp.sum(grad_heads.astype(jnp.float32) * attn_out.astype(jnp.float32), axis=-1)
    grad_values = jnp.einsum(
        "hqk,qhd->kd", prob_low, grad_heads, preferred_element_type=jnp.float32
    )
    grad_prob = jnp.einsum(
        "qhd,kd->hqk", grad_heads, value_local, preferred_element_type=jnp.float32
    )
    grad_score = (attn_prob * (grad_prob - jnp.transpose(deltas)[:, :, None]) * scale).astype(
        jnp.bfloat16
    )
    grad_queries = jnp.einsum(
        "hqk,kd->qhd", grad_score, key_local, preferred_element_type=jnp.float32
    ).astype(jnp.bfloat16)
    grad_keys = jnp.einsum(
        "hqk,qhd->kd", grad_score, query_heads, preferred_element_type=jnp.float32
    )
    partner_keys, partner_values = (
        from_partner(grad_keys.astype(jnp.bfloat16), "tensor", 0).astype(grad_keys.dtype),
        from_partner(grad_values.astype(jnp.bfloat16), "tensor", 0).astype(grad_values.dtype),
    )
    keys_total = (grad_keys + partner_keys).astype(jnp.bfloat16)
    values_total = (grad_values + partner_values).astype(jnp.bfloat16)
    weight_grad = weight_rows / lax.axis_size("dp")
    return (
        grad_queries.reshape(1, length, width),
        keys_total[None],
        values_total[None],
        weight_grad,
    )


def solution(mesh):
    in_specs = (
        P("dp", "tensor", None),
        P("dp", "tensor"),
        P("dp", None, "tensor"),
        P("dp", None, "tensor"),
        P("dp", None, "tensor"),
        P("dp", None),
    )
    out_specs = (
        P("dp", None, "tensor"),
        P("dp", None, "tensor"),
        P("dp", None, "tensor"),
        P("dp", "tensor"),
    )
    return jax.shard_map(local, mesh=mesh, in_specs=in_specs, out_specs=out_specs, check_vma=False)
```

profile of v0, /device:TPU:0, one launch (start us, length us, event | category | flops | bytes accessed | tf_op | source)
XLA Modules:
  0.0 143.6 jit_solution(18421356278678418032)
XLA Ops:
  7.2 0.0 copy-start
  7.2 0.0 all-gather.6.cloned.1.call-start
  7.2 0.7 all-gather.6.cloned.1.call-update
  7.9 0.0 all-gather.4.cloned.1.call-start
  8.0 0.7 all-gather.4.cloned.1.call-update
  8.7 0.0 reduce-scatter.2.cloned.1.call-start
  8.7 0.9 reshape_squeeze.3
  9.7 0.9 fusion.16
  10.5 0.0 copy-done
  10.5 0.3 fusion.55
  10.9 0.0 copy-start.2
  10.9 47.4 %all-gather.6.cloned.1.call-done = bf16[1,256,4096]{2,1,0:T(8,128)(2,1)} async-done(((bf16[1,64,4096]{2,1,0:T(8,128)(2,1)}), bf16[1,256,4096]{2,1,0:T(8,128)(2,1)}) %all-gather.6.cloned.1.call-update) | async-done | bytes 2097168 | tf_op jit(solution)/shard_map/all_gather | solution.py:45
  58.3 28.5 %all-gather.4.cloned.1.call-done = bf16[4096,256]{1,0:T(8,128)(2,1)} async-done(((bf16[512,256]{1,0:T(8,128)(2,1)}), bf16[4096,256]{1,0:T(8,128)(2,1)}) %all-gather.4.cloned.1.call-update) | async-done | bytes 2097168 | tf_op jit(solution)/shard_map/all_gather | solution.py:49
  86.8 3.1 %fusion.13 = bf16[256,256]{0,1:T(8,128)(2,1)S(1)} fusion(bf16[4096,256]{1,0:T(8,128)(2,1)} %all-gather.4.cloned.1.call-done, bf16[1,256,4096]{2,1,0:T(8,128)(2,1)} %all-gather.6.cloned.1.call-done), kind=kOutput, calls=%fused_computation.18 | convolution fusion | flops 536936448 | bytes 4325376 | tf_op jit(solution)/shard_map/dot_general | solution.py:47
  89.9 0.0 copy-start.1
  89.9 0.0 copy-done.2
  90.0 0.5 multiply_reduce_fusion
  90.5 1.0 copy-done.1
  91.5 2.1 %fusion.1 = bf16[4096,256]{0,1:T(8,128)(2,1)} fusion(bf16[256,256]{0,1:T(8,128)(2,1)S(1)} %bitcast.105, bf16[1,256,4096]{2,1,0:T(8,128)(2,1)S(1)} %copy-done.1), kind=kOutput, calls=%fused_computation.2 | convolution fusion | flops 537919488 | bytes 4325376 | tf_op jit(solution)/shard_map/dot_general | solution.py:54
  93.6 0.0 reduce-scatter.2.cloned.1.call-update
  93.6 0.2 fusion.12
  93.8 0.2 fusion.64
  94.1 1.5 %collective-permute-start = (bf16[256,128]{1,0:T(8,128)(2,1)S(1)}, bf16[256,128]{1,0:T(8,128)(2,1)S(1)}, u32[]{:S(2)}, u32[]{:S(2)}) collective-permute-start(bf16[256,128]{1,0:T(8,128)(2,1)S(1)} %get-tuple-element.12), channel_id=1, source_target_pairs={{0,1},{1,0},{2,3},{3,2},{4,5},{5,4},{6,7},{7,6},{8,9},{9,8},{10,11... | collective-permute-start | bytes 196616 | tf_op jit(solution)/shard_map/ppermute | solution.py:16
  95.6 0.2 convolution_convert_fusion.1
  95.8 0.5 fusion.65
  96.4 0.8 copy.19
  97.1 0.5 collective-permute-start.1
  97.7 0.7 collective-permute-done
  98.4 0.6 fusion.20
  99.0 2.3 %collective-permute-done.1 = bf16[256,128]{1,0:T(8,128)(2,1)S(1)} collective-permute-done((bf16[256,128]{1,0:T(8,128)(2,1)S(1)}, bf16[256,128]{1,0:T(8,128)(2,1)S(1)}, u32[]{:S(2)}, u32[]{:S(2)}) %collective-permute-start.1) | collective-permute-done | bytes 65568 | tf_op jit(solution)/shard_map/ppermute | solution.py:16
  101.4 0.6 fusion.21
  102.0 33.0 %reduce-scatter.2.cloned.1.call-done = bf16[512,256]{0,1:T(8,128)(2,1)} async-done(((bf16[4096,256]{0,1:T(8,128)(2,1)}), bf16[512,256]{0,1:T(8,128)(2,1)}) %reduce-scatter.2.cloned.1.call-update) | async-done | bytes 262160 | tf_op jit(solution)/shard_map/reduce_scatter | solution.py:53
  135.0 1.0 convert_multiply_fusion
  136.0 1.0 copy.20
Async XLA Ops:
  7.2 3.4 %copy-start = (bf16[1,256,128]{2,1,0:T(8,128)(2,1)S(1)}, bf16[1,256,128]{2,1,0:T(8,128)(2,1)}, u32[]{:S(2)}) copy-start(bf16[1,256,128]{2,1,0:T(8,128)(2,1)} %param.9) | copy-start | bytes 196612
  7.2 51.1 %all-gather.6.cloned.1.call-start = ((), (), s32[]{:S(2)}) async-start(), calls=%async_computation.3 | async-start | bytes 2621440 | tf_op jit(solution)/shard_map/all_gather | solution.py:45
  7.9 78.9 %all-gather.4.cloned.1.call-start = ((), (), s32[]{:S(2)}) async-start(), calls=%async_computation.1 | async-start | bytes 2359296 | tf_op jit(solution)/shard_map/all_gather | solution.py:49
  8.7 126.3 %reduce-scatter.2.cloned.1.call-start = ((), (), s32[]{:S(2)}) async-start(), calls=%async_computation.2 | async-start | bytes 2359296 | tf_op jit(solution)/shard_map/reduce_scatter | solution.py:53
  10.9 79.1 %copy-start.2 = (bf16[1,256,128]{2,1,0:T(8,128)(2,1)S(1)}, bf16[1,256,128]{2,1,0:T(8,128)(2,1)}, u32[]{:S(2)}) copy-start(bf16[1,256,128]{2,1,0:T(8,128)(2,1)} %param.10) | copy-start | bytes 196612
  89.9 1.6 %copy-start.1 = (bf16[1,256,4096]{2,1,0:T(8,128)(2,1)S(1)}, bf16[1,256,4096]{2,1,0:T(8,128)(2,1)}, u32[]{:S(2)}) copy-start(bf16[1,256,4096]{2,1,0:T(8,128)(2,1)} %all-gather.6.cloned.1.call-done) | copy-start | bytes 6291460
  94.1 4.3 %collective-permute-start = (bf16[256,128]{1,0:T(8,128)(2,1)S(1)}, bf16[256,128]{1,0:T(8,128)(2,1)S(1)}, u32[]{:S(2)}, u32[]{:S(2)}) collective-permute-start(bf16[256,128]{1,0:T(8,128)(2,1)S(1)} %get-tuple-element.12), channel_id=1, source_target_pairs={{0,1},{1,0},{2,3},{3,2},{4,5},{5,4},{6,7},{7,6},{8,9},{9,8},{10,11... | collective-permute-start | bytes 196616 | tf_op jit(solution)/shard_map/ppermute | solution.py:16
  97.1 4.3 %collective-permute-start.1 = (bf16[256,128]{1,0:T(8,128)(2,1)S(1)}, bf16[256,128]{1,0:T(8,128)(2,1)S(1)}, u32[]{:S(2)}, u32[]{:S(2)}) collective-permute-start(bf16[256,128]{1,0:T(8,128)(2,1)S(1)} %get-tuple-element.14), channel_id=1, source_target_pairs={{0,1},{1,0},{2,3},{3,2},{4,5},{5,4},{6,7},{7,6},{8,9},{9,8},{10,11... | collective-permute-start | bytes 196616 | tf_op jit(solution)/shard_map/ppermute | solution.py:16
Sparse Core Ops, SparseCore 0:
  9.6 48.6 all-gather.5
  60.1 26.5 all-gather.3
  93.7 41.2 reduce-scatter.1
where the time goes:
time: 144 us
  waiting for transfers between devices  113 us (78%)
  between operations  13.8 us (10%)
  matrix products  7.24 us (5%)
  local copies, waits for them, and re-layouts  3.77 us (3%)
  other arithmetic  3.15 us (2%)
  starting transfers between devices  2.2 us (2%)
    all_gather x1, waiting for transfers between devices, local(): grad_full = lax.all_gather(grad_local, 'tensor', axis=0, tiled=True)  47.4 us
    reduce_scatter x1, waiting for transfers between devices, local(): lax.psum_scatter(lax.dot_general(columns, flat_out, (((0,), (0,)), ((), (...  33 us
    all_gather x1, waiting for transfers between devices, local(): lax.all_gather(out_weight, 'dp', axis=0, tiled=True)  28.5 us
    dot_general x1, matrix products, local(): jnp.dot(columns, lax.all_gather(out_weight, 'dp', axis=0, tiled=True), pr...  3.15 us
    ppermute x2, waiting for transfers between devices, from_partner(): return lax.ppermute(block, axis, route)  3.08 us
  transfers between devices with their start and end apart: 5, of which 5 were waited for; matrix products, arithmetic and copies ran while one was open for 4% of the time, Pallas kernels for 0%

commit v1 on v0

v1 whole, which is shorter than its diff:
```python
import functools

import jax
import jax.numpy as jnp
from jax import lax
from jax.experimental import pallas as pl
from jax.experimental.pallas import tpu as pltpu
from jax.sharding import PartitionSpec as P

HD = 128
MESH = pl.DeviceIdType.MESH
F32 = jnp.float32
BF16 = jnp.bfloat16
ROWS = 256


def dot(a, b, ca, cb):
    return lax.dot_general(a, b, (((ca,), (cb,)), ((), ())), preferred_element_type=F32)


def kernel(
    nchip, n, grad_ref, weight_ref, q_ref, k_ref, v_ref, seg_ref,
    dq_ref, dk_ref, dv_ref, dw_ref,
    og, wfull, prob, seg_col, attn, gsum, kv_send, kv_recv,
    xsend, xrecv, part, rs_send, rs_recv,
    fill_sem, wfill_sem, rsend_sem, rrecv_sem, lsend_sem, lrecv_sem,
    wsend_sem, wrecv_sem, wxsend_sem, wxrecv_sem,
    xsend_sem, xrecv_sem, rss_sem, rsr_sem, kvs_sem, kvr_sem,
):
    d = lax.axis_index("dp")
    t = lax.axis_index("tensor")
    chip, core = d // 2, d % 2
    sibling = (chip * 2 + 1 - core, t)
    partner = (d, t + 1 - 2 * (t % 2))
    length, width = q_ref.shape
    depth = weight_ref.shape[0]
    heads = width // HD
    scale = HD ** (-0.5)
    has_left, has_right = t > 0, t < n - 1

    def behind(p):
        return lax.rem(chip - 1 - p + 2 * nchip, nchip)

    def ahead(p):
        return lax.rem(chip + 1 + p, nchip)

    def fill(j):
        return pltpu.make_async_copy(
            grad_ref.at[:, pl.ds(j * 2 * depth, 2 * depth)], og.at[j, t], fill_sem.at[j]
        )

    def wfill():
        return pltpu.make_async_copy(weight_ref, wfull.at[chip, core], wfill_sem)

    def go_right(p, s):
        at = og.at[behind(p), lax.rem(t - s + 1 + n, n)]
        return pltpu.make_async_remote_copy(
            at, at, rsend_sem.at[p, s - 1], rrecv_sem.at[p, s - 1],
            device_id=(d, lax.rem(t + 1, n)), device_id_type=MESH)

    def from_left(p, s):
        at = og.at[behind(p), lax.rem(t - s + n, n)]
        return pltpu.make_async_remote_copy(
            at, at, rsend_sem.at[p, s - 1], rrecv_sem.at[p, s - 1],
            device_id=(d, lax.rem(t + 1, n)), device_id_type=MESH)

    def go_left(p, s):
        at = og.at[behind(p), lax.rem(t + s - 1, n)]
        return pltpu.make_async_remote_copy(
            at, at, lsend_sem.at[p, s - 1], lrecv_sem.at[p, s - 1],
            device_id=(d, lax.rem(t - 1 + n, n)), device_id_type=MESH)

    def from_right(p, s):
        at = og.at[behind(p), lax.rem(t + s, n)]
        return pltpu.make_async_remote_copy(
            at, at, lsend_sem.at[p, s - 1], lrecv_sem.at[p, s - 1],
            device_id=(d, lax.rem(t - 1 + n, n)), device_id_type=MESH)

    def w_out(p):
        at = wfull.at[chip, core]
        return pltpu.make_async_remote_copy(
            at, at, wsend_sem.at[p], wrecv_sem.at[p],
            device_id=(ahead(p) * 2 + core, t), device_id_type=MESH)

    def w_in(p):
        at = wfull.at[behind(p), core]
        return pltpu.make_async_remote_copy(
            at, at, wsend_sem.at[p], wrecv_sem.at[p],
            device_id=(ahead(p) * 2 + core, t), device_id_type=MESH)

    def w_across(p):
        at = wfull.at[behind(p), core]
        return pltpu.make_async_remote_copy(
            at, at, wxsend_sem.at[p], wxrecv_sem.at[p], device_id=sibling, device_id_type=MESH)

    def w_from_sibling(p):
        at = wfull.at[behind(p), 1 - core]
        return pltpu.make_async_remote_copy(
            at, at, wxsend_sem.at[p], wxrecv_sem.at[p], device_id=sibling, device_id_type=MESH)

    def x_copy(p):
        return pltpu.make_async_remote_copy(
            xsend.at[p], xrecv.at[p], xsend_sem.at[p], xrecv_sem.at[p],
            device_id=sibling, device_id_type=MESH)

    def rs_copy(p):
        return pltpu.make_async_remote_copy(
            rs_send.at[p], rs_recv.at[p], rss_sem.at[p], rsr_sem.at[p],
            device_id=(behind(p) * 2 + core, t), device_id_type=MESH)

    def kv_copy():
        return pltpu.make_async_remote_copy(
            kv_send, kv_recv, kvs_sem, kvr_sem, device_id=partner, device_id_type=MESH)

    def send_own(p):
        @pl.when(has_right)
        def _():
            go_right(p, 1).start()

        @pl.when(has_left)
        def _():
            go_left(p, 1).start()

    for j in range(nchip):
        fill(j).start()
    wfill().start()

    barrier = pltpu.get_barrier_semaphore()

    @pl.when(has_left)
    def _():
        pl.semaphore_signal(barrier, 1, device_id=(d, lax.rem(t - 1 + n, n)), device_id_type=MESH)

    @pl.when(has_right)
    def _():
        pl.semaphore_signal(barrier, 1, device_id=(d, lax.rem(t + 1, n)), device_id_type=MESH)

    pl.semaphore_signal(barrier, 1, device_id=sibling, device_id_type=MESH)
    for p in range(nchip - 1):
        pl.semaphore_signal(barrier, 1, device_id=(ahead(p) * 2 + core, t), device_id_type=MESH)
    inner = has_left & has_right

    @pl.when(inner)
    def _():
        pl.semaphore_wait(barrier, nchip + 2)

    @pl.when(jnp.logical_not(inner))
    def _():
        pl.semaphore_wait(barrier, nchip + 1)

    for j in range(nchip):
        fill(j).wait()
    wfill().wait()
    send_own(0)
    for p in range(nchip - 1):
        w_out(p).start()
    w_across(nchip - 1).start()

    seg_col[...] = jnp.transpose(jnp.broadcast_to(seg_ref[...], (128, length)))
    rows = min(ROWS, length)
    blocks = length // rows

    def row_block(b):
        return pl.ds(pl.multiple_of(b * rows, rows), rows)

    def forward(b, carry):
        at = row_block(b)
        same = seg_col[at, :][:, :1] == seg_ref[...]
        row = lax.broadcasted_iota(jnp.int32, (rows, length), 0) + b * rows
        col = lax.broadcasted_iota(jnp.int32, (rows, length), 1)
        visible = same & (row >= col)
        for h in range(heads):
            cols = slice(h * HD, (h + 1) * HD)
            scores = dot(q_ref[at, cols], k_ref[...], 1, 1) * scale
            masked = jnp.where(visible, scores, -jnp.inf)
            raw = jnp.exp(masked - jnp.max(masked, axis=-1, keepdims=True))
            p_full = raw / jnp.sum(raw, axis=-1, keepdims=True)
            prob[h, at, :] = p_full
            attn[at, cols] = dot(p_full.astype(BF16), v_ref[...], 1, 0).astype(BF16)
        return carry

    lax.fori_loop(0, blocks, forward, 0)
    gsum[...] = jnp.zeros_like(gsum)

    def weight_term(p, which):
        cols = pl.ds(pl.multiple_of(which * depth, depth), depth)
        block = og[behind(p), :, :, cols].reshape(length, depth)
        return dot(block, attn[...], 0, 0).astype(BF16)

    def weight_terms(p):
        xsend[p] = weight_term(p, 1 - core)
        x_copy(p).start()
        part[p] = weight_term(p, core)

    def step(i, carry):
        @pl.when(i + 1 < nchip)
        def _():
            send_own(i + 1)

        done = i - (n - 1)

        @pl.when(done >= 0)
        def _():
            x_copy(done).wait_recv()
            rs_send[done] = (part[done].astype(F32) + xrecv[done].astype(F32)).astype(BF16)
            rs_copy(done).start()

        for s in range(1, n):
            p = i - (s - 1)
            live = (p >= 0) & (p < nchip)

            @pl.when(live & (t >= s))
            def _():
                from_left(p, s).wait_recv()

            @pl.when(live & (t + s < n))
            def _():
                from_right(p, s).wait_recv()

            if s < n - 1:
                @pl.when(live & (t >= s) & has_right)
                def _():
                    go_right(p, s + 1).start()

                @pl.when(live & (t + s < n) & has_left)
                def _():
                    go_left(p, s + 1).start()

        early = i - max(n - 3, 0)

        @pl.when((early >= 0) & (early < nchip - 1))
        def _():
            w_in(early).wait_recv()
            w_across(early).start()

        now = i - (n - 2)

        @pl.when(now >= 0)
        def _():
            w_from_sibling(now).wait_recv()
            j = behind(now)
            gsum[...] += dot(
                og[j].reshape(length, 2 * depth), wfull[j].reshape(2 * depth, width), 1, 0)

            @pl.when(now < nchip - 1)
            def _():
                weight_terms(now)

        return carry

    lax.fori_loop(0, nchip + n - 2, step, 0)

    dk_sum = jnp.zeros((length, HD), F32)
    dv_sum = jnp.zeros((length, HD), F32)

    def backward(b, carry):
        dk_sum, dv_sum = carry
        at = row_block(b)
        for h in range(heads):
            cols = slice(h * HD, (h + 1) * HD)
            gh = gsum[at, cols].astype(BF16)
            p_full = prob[h, at, :]
            delta = jnp.sum(
                gh.astype(F32) * attn[at, cols].astype(F32), axis=-1, keepdims=True)
            dv_sum = dv_sum + dot(p_full.astype(BF16), gh, 0, 0)
            gs = (p_full * (dot(gh, v_ref[...], 1, 1) - delta) * scale).astype(BF16)
            dk_sum = dk_sum + dot(gs, q_ref[at, cols], 0, 0)
            dq_ref[at, cols] = dot(gs, k_ref[...], 1, 0).astype(BF16)
        return dk_sum, dv_sum

    if blocks == 1:
        dk_sum, dv_sum = backward(0, (dk_sum, dv_sum))
    else:
        dk_sum, dv_sum = lax.fori_loop(0, blocks, backward, (dk_sum, dv_sum))
    kv_send[0] = dk_sum.astype(BF16)
    kv_send[1] = dv_sum.astype(BF16)
    kv_copy().start()
    last = nchip - 1
    weight_terms(last)
    kv_copy().wait_recv()
    dk_ref[...] = (dk_sum + kv_recv[0].astype(F32)).astype(BF16)
    dv_ref[...] = (dv_sum + kv_recv[1].astype(F32)).astype(BF16)

    x_copy(last).wait_recv()
    total = part[last].astype(F32) + xrecv[last].astype(F32)
    for p in range(nchip - 1):
        rs_copy(p).wait_recv()
        total = total + rs_recv[p].astype(F32)
    dw_ref[...] = total * (1.0 / (2 * nchip))

    kv_copy().wait_send()

    def drain(p, carry):
        x_copy(p).wait_send()
        w_across(p).wait_send()

        @pl.when(p < nchip - 1)
        def _():
            w_out(p).wait_send()
            rs_copy(p).wait_send()

        for s in range(1, n):
            @pl.when(has_right & (t >= s - 1))
            def _():
                go_right(p, s).wait_send()

            @pl.when(has_left & (t + s - 1 < n))
            def _():
                go_left(p, s).wait_send()

        return carry

    lax.fori_loop(0, nchip, drain, 0)


def local(nchip, n, out_grad, out_weight, queries, keys, values, segment_ids):
    grad, q, k, v = out_grad[0], queries[0], keys[0], values[0]
    rows, model = grad.shape
    depth, width = out_weight.shape
    length = q.shape[0]
    heads = width // HD
    vmem = pl.BlockSpec(memory_space=pltpu.VMEM)
    hbm = pl.BlockSpec(memory_space=pl.ANY)
    dma = pltpu.SemaphoreType.DMA
    most = max(nchip - 1, 1)
    dq, dk, dv, dw = pl.pallas_call(
        functools.partial(kernel, nchip, n),
        out_shape=(
            jax.ShapeDtypeStruct((length, width), BF16),
            jax.ShapeDtypeStruct((length, HD), BF16),
            jax.ShapeDtypeStruct((length, HD), BF16),
            jax.ShapeDtypeStruct((depth, width), F32),
        ),
        in_specs=[hbm, hbm, vmem, vmem, vmem, vmem],
        out_specs=(vmem, vmem, vmem, vmem),
        scratch_shapes=[
            pltpu.VMEM((nchip, n, rows, 2 * depth), BF16),
            pltpu.VMEM((nchip, 2, depth, width), BF16),
            pltpu.VMEM((heads, length, length), F32),
            pltpu.VMEM((length, 128), jnp.int32),
            pltpu.VMEM((length, width), BF16),
            pltpu.VMEM((length, width), F32),
            pltpu.VMEM((2, length, HD), BF16),
            pltpu.VMEM((2, length, HD), BF16),
            pltpu.VMEM((nchip, depth, width), BF16),
            pltpu.VMEM((nchip, depth, width), BF16),
            pltpu.VMEM((nchip, depth, width), BF16),
            pltpu.VMEM((most, depth, width), BF16),
            pltpu.VMEM((most, depth, width), BF16),
            dma((nchip,)), dma,
            dma((nchip, n - 1)), dma((nchip, n - 1)), dma((nchip, n - 1)), dma((nchip, n - 1)),
            dma((most,)), dma((most,)), dma((nchip,)), dma((nchip,)),
            dma((nchip,)), dma((nchip,)), dma((most,)), dma((most,)),
            dma, dma,
        ],
        compiler_params=pltpu.CompilerParams(
            collective_id=0, has_side_effects=True, vmem_limit_bytes=56 << 20),
        cost_estimate=pl.CostEstimate(
            flops=4 * length * model * width, bytes_accessed=8 << 20, transcendentals=0),
    )(grad, out_weight, q, k, v, segment_ids)
    return dq[None], dk[None], dv[None], dw


def solution(mesh):
    in_specs = (
        P("dp", "tensor", None),
        P("dp", "tensor"),
        P("dp", None, "tensor"),
        P("dp", None, "tensor"),
        P("dp", None, "tensor"),
        P("dp", None),
    )
    out_specs = (
        P("dp", None, "tensor"),
        P("dp", None, "tensor"),
        P("dp", None, "tensor"),
        P("dp", "tensor"),
    )
    body = functools.partial(local, mesh.shape["dp"] // 2, mesh.shape["tensor"])
    return jax.shard_map(body, mesh=mesh, in_specs=in_specs, out_specs=out_specs, check_vma=False)
```

time: 144 us -> 56.5 us (0.39)
  waiting for transfers between devices: 113 us -> 0 us
  Pallas kernels: 0 us -> 50.3 us
  between operations: 13.8 us -> 0.65 us
  matrix products: 7.24 us -> 0 us
  other arithmetic: 3.15 us -> 0 us
  starting transfers between devices: 2.2 us -> 0 us
  local copies, waits for them, and re-layouts: 3.77 us -> 5.37 us
    all_gather x2 -> x0, waiting for transfers between devices: 75.9 us -> none  [the longest x1 47.4 us: local(): grad_full = lax.all_gather(grad_local, 'tensor', axis=0, tiled=True)]
    pallas_call x0 -> x1, Pallas kernels: none -> 50.3 us  [local(): pl.pallas_call(functools.partial(kernel, nchip, n), out_shape=(jax.ShapeD...]
    reduce_scatter x1 -> x0, waiting for transfers between devices: 33 us -> none  [local(): lax.psum_scatter(lax.dot_general(columns, flat_out, (((0,), (0,)), ((), (...]
    dot_general x7 -> x0, matrix products: 6.89 us -> none  [the longest x1 3.15 us: local(): jnp.dot(columns, lax.all_gather(out_weight, 'dp', axis=0, tiled=True), pr...]
    ppermute x2 -> x0, waiting for transfers between devices: 3.08 us -> none  [from_partner(): return lax.ppermute(block, axis, route)]
    unnamed x8 -> x6, local copies, waits for them, and re-layouts: 2.83 us -> 5.37 us
    ppermute x2 -> x0, starting transfers between devices: 2.09 us -> none  [from_partner(): return lax.ppermute(block, axis, route)]
  transfers between devices with their start and end apart: 5 -> 0, of which waited for: 5 -> 0; matrix products, arithmetic and copies ran while one was open for 4% -> 0% of each run, Pallas kernels for 0% -> 0%
where the time goes in v1:
time: 56.5 us; the launch traced here: 56.3 us
  Pallas kernels  50.3 us (89%)
  local copies, waits for them, and re-layouts  5.37 us (10%)
  between operations  0.65 us (1%)
    pallas_call x1, Pallas kernels, local(): pl.pallas_call(functools.partial(kernel, nchip, n), out_shape=(jax.ShapeD...  50.3 us
    unnamed x6, local copies, waits for them, and re-layouts  5.37 us

profile of v1, /device:TPU:0, one launch (start us, length us, event | category | flops | bytes accessed | tf_op | source)
XLA Modules:
  0.0 56.3 jit_solution(8468911596056653839)
XLA Ops:
  0.6 50.3 %shard_map.93 = (bf16[256,256]{1,0:T(8,128)(2,1)}, bf16[256,128]{1,0:T(8,128)(2,1)}, bf16[256,128]{1,0:T(8,128)(2,1)}, f32[512,256]{1,0:T(8,128)}) custom-call(bf16[64,4096]{1,0:T(8,128)(2,1)} %bitcast.10, bf16[512,256]{1,0:T(8,128)(2,1)} %weight_ref.1, bf16[256,256]{1,0:T(8,128)(2,1)} %bitcast.11, bf16[256,128]{1,0:T(8,128)(2,1)} %bitcast.12, ...), custom_call_target="tpu_custom_call" | custom-call | flops 1073741824 | bytes 8388608 | tf_op jit(solution)/shard_map/pallas_call | solution.py:326
  50.9 0.0 copy-start
  50.9 1.6 %copy.14 = bf16[1,256,256]{2,1,0:T(8,128)(2,1)} copy(bf16[1,256,256]{2,1,0:T(8,128)(2,1)} %bitcast.7) | data formatting | bytes 262144
  52.6 1.5 %copy.15 = bf16[1,256,128]{2,1,0:T(8,128)(2,1)} copy(bf16[1,256,128]{2,1,0:T(8,128)(2,1)} %bitcast.9) | data formatting | bytes 131072
  54.0 1.5 %copy.16 = bf16[1,256,128]{2,1,0:T(8,128)(2,1)} copy(bf16[1,256,128]{2,1,0:T(8,128)(2,1)} %bitcast.8) | data formatting | bytes 131072
  55.5 0.0 copy-done
  55.5 0.8 %copy.17 = f32[512,256]{1,0:T(8,128)} copy(f32[512,256]{1,0:T(8,128)S(1)} %copy-done) | data formatting | bytes 1048576
Async XLA Ops:
  50.9 4.6 %copy-start = (f32[512,256]{1,0:T(8,128)S(1)}, f32[512,256]{1,0:T(8,128)}, u32[]{:S(2)}) copy-start(f32[512,256]{1,0:T(8,128)} %get-tuple-element.19) | copy-start | bytes 1572868

commit v2 on v1

--- a/solution.py
+++ b/solution.py
@@ -313,6 +313,17 @@
     lax.fori_loop(0, nchip, drain, 0)
 
 
+def hand_out(*refs):
+    sources, results, sems = refs[:4], refs[4:8], refs[8]
+    copies = [
+        pltpu.make_async_copy(a, b, sems.at[i]) for i, (a, b) in enumerate(zip(sources, results))
+    ]
+    for copy in copies:
+        copy.start()
+    for copy in copies:
+        copy.wait()
+
+
 def local(nchip, n, out_grad, out_weight, queries, keys, values, segment_ids):
     grad, q, k, v = out_grad[0], queries[0], keys[0], values[0]
     rows, model = grad.shape
@@ -323,7 +334,7 @@
     hbm = pl.BlockSpec(memory_space=pl.ANY)
     dma = pltpu.SemaphoreType.DMA
     most = max(nchip - 1, 1)
-    dq, dk, dv, dw = pl.pallas_call(
+    results = pl.pallas_call(
         functools.partial(kernel, nchip, n),
         out_shape=(
             jax.ShapeDtypeStruct((length, width), BF16),
@@ -358,6 +369,13 @@
         cost_estimate=pl.CostEstimate(
             flops=4 * length * model * width, bytes_accessed=8 << 20, transcendentals=0),
     )(grad, out_weight, q, k, v, segment_ids)
+    dq, dk, dv, dw = pl.pallas_call(
+        hand_out,
+        out_shape=tuple(jax.ShapeDtypeStruct(r.shape, r.dtype) for r in results),
+        in_specs=[hbm] * 4,
+        out_specs=(hbm,) * 4,
+        scratch_shapes=[dma((4,))],
+    )(*results)
     return dq[None], dk[None], dv[None], dw
 
 

time: 56.5 us -> 76 us (1.35)
  Pallas kernels: 50.3 us -> 75.2 us
  local copies, waits for them, and re-layouts: 5.37 us -> 0 us
    pallas_call x0 -> x1, Pallas kernels: none -> 25 us  [local(): pl.pallas_call(hand_out, out_shape=tuple((jax.ShapeDtypeStruct(r.shape, r...]
    unnamed x6 -> x0, local copies, waits for them, and re-layouts: 5.37 us -> none
where the time goes in v2:
time: 76 us; the launch traced here: 75.9 us
  Pallas kernels  75.2 us (99%)
    pallas_call x1, Pallas kernels, local(): pl.pallas_call(functools.partial(kernel, nchip, n), out_shape=(jax.ShapeD...  50.3 us
    pallas_call x1, Pallas kernels, local(): pl.pallas_call(hand_out, out_shape=tuple((jax.ShapeDtypeStruct(r.shape, r...  25 us

profile of v2, /device:TPU:0, one launch (start us, length us, event | category | flops | bytes accessed | tf_op | source)
XLA Modules:
  0.0 75.9 jit_solution(11041079611238881547)
XLA Ops:
  0.6 50.3 %shard_map.93 = (bf16[256,256]{1,0:T(8,128)(2,1)}, bf16[256,128]{1,0:T(8,128)(2,1)}, bf16[256,128]{1,0:T(8,128)(2,1)}, f32[512,256]{1,0:T(8,128)}) custom-call(bf16[64,4096]{1,0:T(8,128)(2,1)} %bitcast.7, bf16[512,256]{1,0:T(8,128)(2,1)} %weight_ref.1, bf16[256,256]{1,0:T(8,128)(2,1)} %bitcast.8, bf16[256,128]{1,0:T(8,128)(2,1)} %bitcast.10, ...), custom_call_target="tpu_custom_call" | custom-call | flops 1073741824 | bytes 8388608 | tf_op jit(solution)/shard_map/pallas_call | solution.py:337
  50.9 25.0 %shard_map.94 = (bf16[256,256]{1,0:T(8,128)(2,1)}, bf16[256,128]{1,0:T(8,128)(2,1)}, bf16[256,128]{1,0:T(8,128)(2,1)}, f32[512,256]{1,0:T(8,128)}) custom-call(bf16[256,256]{1,0:T(8,128)(2,1)} %get-tuple-element.12.refs_0_, bf16[256,128]{1,0:T(8,128)(2,1)} %get-tuple-element.13.refs_1_, bf16[256,128]{1,0:T(8,128)(2,1)} %get-tuple-element.14.refs_2_, ...), custom_call_target="tpu_custom_call" | custom-call | tf_op jit(solution)/shard_map/pallas_call | solution.py:372

commit v3 on v1

--- a/solution.py
+++ b/solution.py
@@ -313,6 +313,11 @@
     lax.fori_loop(0, nchip, drain, 0)
 
 
+def hand_out(*refs):
+    for source, result in zip(refs[:4], refs[4:]):
+        result[...] = source[...]
+
+
 def local(nchip, n, out_grad, out_weight, queries, keys, values, segment_ids):
     grad, q, k, v = out_grad[0], queries[0], keys[0], values[0]
     rows, model = grad.shape
@@ -323,7 +328,7 @@
     hbm = pl.BlockSpec(memory_space=pl.ANY)
     dma = pltpu.SemaphoreType.DMA
     most = max(nchip - 1, 1)
-    dq, dk, dv, dw = pl.pallas_call(
+    results = pl.pallas_call(
         functools.partial(kernel, nchip, n),
         out_shape=(
             jax.ShapeDtypeStruct((length, width), BF16),
@@ -358,6 +363,12 @@
         cost_estimate=pl.CostEstimate(
             flops=4 * length * model * width, bytes_accessed=8 << 20, transcendentals=0),
     )(grad, out_weight, q, k, v, segment_ids)
+    dq, dk, dv, dw = pl.pallas_call(
+        hand_out,
+        out_shape=tuple(jax.ShapeDtypeStruct(r.shape, r.dtype) for r in results),
+        in_specs=[vmem] * 4,
+        out_specs=(vmem,) * 4,
+    )(*results)
     return dq[None], dk[None], dv[None], dw
 
 

time: 56.5 us -> 53.1 us (0.940)
  local copies, waits for them, and re-layouts: 5.37 us -> 0 us
  Pallas kernels: 50.3 us -> 52.3 us
    unnamed x6 -> x0, local copies, waits for them, and re-layouts: 5.37 us -> none
    pallas_call x0 -> x1, Pallas kernels: none -> 2.06 us  [local(): pl.pallas_call(hand_out, out_shape=tuple((jax.ShapeDtypeStruct(r.shape, r...]
where the time goes in v3:
time: 53.1 us; the launch traced here: 53 us
  Pallas kernels  52.3 us (98%)
  between operations  0.64 us (1%)
    pallas_call x1, Pallas kernels, local(): pl.pallas_call(functools.partial(kernel, nchip, n), out_shape=(jax.ShapeD...  50.3 us
    pallas_call x1, Pallas kernels, local(): pl.pallas_call(hand_out, out_shape=tuple((jax.ShapeDtypeStruct(r.shape, r...  2.06 us

profile of v3, /device:TPU:0, one launch (start us, length us, event | category | flops | bytes accessed | tf_op | source)
XLA Modules:
  0.0 53.0 jit_solution(13337464384070638651)
XLA Ops:
  0.6 50.3 %shard_map.93 = (bf16[256,256]{1,0:T(8,128)(2,1)}, bf16[256,128]{1,0:T(8,128)(2,1)}, bf16[256,128]{1,0:T(8,128)(2,1)}, f32[512,256]{1,0:T(8,128)}) custom-call(bf16[64,4096]{1,0:T(8,128)(2,1)} %bitcast.7, bf16[512,256]{1,0:T(8,128)(2,1)} %weight_ref.1, bf16[256,256]{1,0:T(8,128)(2,1)} %bitcast.8, bf16[256,128]{1,0:T(8,128)(2,1)} %bitcast.10, ...), custom_call_target="tpu_custom_call" | custom-call | flops 1073741824 | bytes 8388608 | tf_op jit(solution)/shard_map/pallas_call | solution.py:331
  50.9 2.1 %shard_map.94 = (bf16[256,256]{1,0:T(8,128)(2,1)}, bf16[256,128]{1,0:T(8,128)(2,1)}, bf16[256,128]{1,0:T(8,128)(2,1)}, f32[512,256]{1,0:T(8,128)}) custom-call(bf16[256,256]{1,0:T(8,128)(2,1)} %get-tuple-element.12.refs_0_, bf16[256,128]{1,0:T(8,128)(2,1)} %get-tuple-element.13.refs_1_, bf16[256,128]{1,0:T(8,128)(2,1)} %get-tuple-element.14.refs_2_, ...), custom_call_target="tpu_custom_call" | custom-call | tf_op jit(solution)/shard_map/pallas_call | solution.py:366

commit v4 on v3

--- a/solution.py
+++ b/solution.py
@@ -44,34 +44,34 @@
     def ahead(p):
         return lax.rem(chip + 1 + p, nchip)
 
-    def fill(j):
+    def fill(c):
         return pltpu.make_async_copy(
-            grad_ref.at[:, pl.ds(j * 2 * depth, 2 * depth)], og.at[j, t], fill_sem.at[j]
+            grad_ref.at[:, pl.ds(c * depth, depth)], og.at[c // 2, c % 2, t], fill_sem.at[c]
         )
 
     def wfill():
         return pltpu.make_async_copy(weight_ref, wfull.at[chip, core], wfill_sem)
 
     def go_right(p, s):
-        at = og.at[behind(p), lax.rem(t - s + 1 + n, n)]
+        at = og.at[behind(p // 2), p % 2, lax.rem(t - s + 1 + n, n)]
         return pltpu.make_async_remote_copy(
             at, at, rsend_sem.at[p, s - 1], rrecv_sem.at[p, s - 1],
             device_id=(d, lax.rem(t + 1, n)), device_id_type=MESH)
 
     def from_left(p, s):
-        at = og.at[behind(p), lax.rem(t - s + n, n)]
+        at = og.at[behind(p // 2), p % 2, lax.rem(t - s + n, n)]
         return pltpu.make_async_remote_copy(
             at, at, rsend_sem.at[p, s - 1], rrecv_sem.at[p, s - 1],
             device_id=(d, lax.rem(t + 1, n)), device_id_type=MESH)
 
     def go_left(p, s):
-        at = og.at[behind(p), lax.rem(t + s - 1, n)]
+        at = og.at[behind(p // 2), p % 2, lax.rem(t + s - 1, n)]
         return pltpu.make_async_remote_copy(
             at, at, lsend_sem.at[p, s - 1], lrecv_sem.at[p, s - 1],
             device_id=(d, lax.rem(t - 1 + n, n)), device_id_type=MESH)
 
     def from_right(p, s):
-        at = og.at[behind(p), lax.rem(t + s, n)]
+        at = og.at[behind(p // 2), p % 2, lax.rem(t + s, n)]
         return pltpu.make_async_remote_copy(
             at, at, lsend_sem.at[p, s - 1], lrecv_sem.at[p, s - 1],
             device_id=(d, lax.rem(t - 1 + n, n)), device_id_type=MESH)
@@ -121,7 +121,7 @@
         def _():
             go_left(p, 1).start()
 
-    for j in range(nchip):
+    for j in range(2 * nchip):
         fill(j).start()
     wfill().start()
 
@@ -148,10 +148,11 @@
     def _():
         pl.semaphore_wait(barrier, nchip + 1)
 
-    for j in range(nchip):
+    for j in range(2 * nchip):
         fill(j).wait()
     wfill().wait()
-    send_own(0)
+    for p in range(min(4, 2 * nchip)):
+        send_own(p)
     for p in range(nchip - 1):
         w_out(p).start()
     w_across(nchip - 1).start()
@@ -183,8 +184,7 @@
     gsum[...] = jnp.zeros_like(gsum)
 
     def weight_term(p, which):
-        cols = pl.ds(pl.multiple_of(which * depth, depth), depth)
-        block = og[behind(p), :, :, cols].reshape(length, depth)
+        block = og[behind(p), which].reshape(length, depth)
         return dot(block, attn[...], 0, 0).astype(BF16)
 
     def weight_terms(p):
@@ -193,21 +193,22 @@
         part[p] = weight_term(p, core)
 
     def step(i, carry):
-        @pl.when(i + 1 < nchip)
-        def _():
-            send_own(i + 1)
-
-        done = i - (n - 1)
-
-        @pl.when(done >= 0)
-        def _():
-            x_copy(done).wait_recv()
-            rs_send[done] = (part[done].astype(F32) + xrecv[done].astype(F32)).astype(BF16)
-            rs_copy(done).start()
+        @pl.when(i + 4 < 2 * nchip)
+        def _():
+            send_own(i + 4)
+
+        done = i - n
+
+        @pl.when((done >= 0) & (done % 2 == 0))
+        def _():
+            p = done // 2
+            x_copy(p).wait_recv()
+            rs_send[p] = (part[p].astype(F32) + xrecv[p].astype(F32)).astype(BF16)
+            rs_copy(p).start()
 
         for s in range(1, n):
             p = i - (s - 1)
-            live = (p >= 0) & (p < nchip)
+            live = (p >= 0) & (p < 2 * nchip)
 
             @pl.when(live & (t >= s))
             def _():
@@ -228,27 +229,31 @@
 
         early = i - max(n - 3, 0)
 
-        @pl.when((early >= 0) & (early < nchip - 1))
-        def _():
-            w_in(early).wait_recv()
-            w_across(early).start()
+        @pl.when((early >= 0) & (early < 2 * (nchip - 1)) & (early % 2 == 0))
+        def _():
+            w_in(early // 2).wait_recv()
+            w_across(early // 2).start()
 
         now = i - (n - 2)
 
         @pl.when(now >= 0)
         def _():
-            w_from_sibling(now).wait_recv()
-            j = behind(now)
-            gsum[...] += dot(
-                og[j].reshape(length, 2 * depth), wfull[j].reshape(2 * depth, width), 1, 0)
-
-            @pl.when(now < nchip - 1)
-            def _():
-                weight_terms(now)
+            p, half = now // 2, now % 2
+
+            @pl.when(half == 0)
+            def _():
+                w_from_sibling(p).wait_recv()
+
+            j = behind(p)
+            gsum[...] += dot(og[j, half].reshape(length, depth), wfull[j, half], 1, 0)
+
+            @pl.when((half == 1) & (p < nchip - 1))
+            def _():
+                weight_terms(p)
 
         return carry
 
-    lax.fori_loop(0, nchip + n - 2, step, 0)
+    lax.fori_loop(0, 2 * nchip + n - 2, step, 0)
 
     dk_sum = jnp.zeros((length, HD), F32)
     dv_sum = jnp.zeros((length, HD), F32)
@@ -299,6 +304,9 @@
             w_out(p).wait_send()
             rs_copy(p).wait_send()
 
+        return carry
+
+    def drain_line(p, carry):
         for s in range(1, n):
             @pl.when(has_right & (t >= s - 1))
             def _():
@@ -310,6 +318,7 @@
 
         return carry
 
+    lax.fori_loop(0, 2 * nchip, drain_line, 0)
     lax.fori_loop(0, nchip, drain, 0)
 
 
@@ -339,7 +348,7 @@
         in_specs=[hbm, hbm, vmem, vmem, vmem, vmem],
         out_specs=(vmem, vmem, vmem, vmem),
         scratch_shapes=[
-            pltpu.VMEM((nchip, n, rows, 2 * depth), BF16),
+            pltpu.VMEM((nchip, 2, n, rows, depth), BF16),
             pltpu.VMEM((nchip, 2, depth, width), BF16),
             pltpu.VMEM((heads, length, length), F32),
             pltpu.VMEM((length, 128), jnp.int32),
@@ -352,8 +361,9 @@
             pltpu.VMEM((nchip, depth, width), BF16),
             pltpu.VMEM((most, depth, width), BF16),
             pltpu.VMEM((most, depth, width), BF16),
-            dma((nchip,)), dma,
-            dma((nchip, n - 1)), dma((nchip, n - 1)), dma((nchip, n - 1)), dma((nchip, n - 1)),
+            dma((2 * nchip,)), dma,
+            dma((2 * nchip, n - 1)), dma((2 * nchip, n - 1)),
+            dma((2 * nchip, n - 1)), dma((2 * nchip, n - 1)),
             dma((most,)), dma((most,)), dma((nchip,)), dma((nchip,)),
             dma((nchip,)), dma((nchip,)), dma((most,)), dma((most,)),
             dma, dma,

time: 53.1 us -> 52 us (0.979)
  Pallas kernels: 52.3 us -> 51.2 us
    pallas_call x1, Pallas kernels: 50.3 us -> 49.1 us  [local(): pl.pallas_call(functools.partial(kernel, nchip, n), out_shape=(jax.ShapeD...]
where the time goes in v4:
time: 52 us; the launch traced here: 51.8 us
  Pallas kernels  51.2 us (98%)
  between operations  0.64 us (1%)
    pallas_call x1, Pallas kernels, local(): pl.pallas_call(functools.partial(kernel, nchip, n), out_shape=(jax.ShapeD...  49.1 us
    pallas_call x1, Pallas kernels, local(): pl.pallas_call(hand_out, out_shape=tuple((jax.ShapeDtypeStruct(r.shape, r...  2.06 us

profile of v4, /device:TPU:0, one launch (start us, length us, event | category | flops | bytes accessed | tf_op | source)
XLA Modules:
  0.0 51.8 jit_solution(7643270118538606036)
XLA Ops:
  0.6 49.1 %shard_map.93 = (bf16[256,256]{1,0:T(8,128)(2,1)}, bf16[256,128]{1,0:T(8,128)(2,1)}, bf16[256,128]{1,0:T(8,128)(2,1)}, f32[512,256]{1,0:T(8,128)}) custom-call(bf16[64,4096]{1,0:T(8,128)(2,1)} %bitcast.7, bf16[512,256]{1,0:T(8,128)(2,1)} %weight_ref.1, bf16[256,256]{1,0:T(8,128)(2,1)} %bitcast.8, bf16[256,128]{1,0:T(8,128)(2,1)} %bitcast.10, ...), custom_call_target="tpu_custom_call" | custom-call | flops 1073741824 | bytes 8388608 | tf_op jit(solution)/shard_map/pallas_call | solution.py:340
  49.8 2.1 %shard_map.94 = (bf16[256,256]{1,0:T(8,128)(2,1)}, bf16[256,128]{1,0:T(8,128)(2,1)}, bf16[256,128]{1,0:T(8,128)(2,1)}, f32[512,256]{1,0:T(8,128)}) custom-call(bf16[256,256]{1,0:T(8,128)(2,1)} %get-tuple-element.12.refs_0_, bf16[256,128]{1,0:T(8,128)(2,1)} %get-tuple-element.13.refs_1_, bf16[256,128]{1,0:T(8,128)(2,1)} %get-tuple-element.14.refs_2_, ...), custom_call_target="tpu_custom_call" | custom-call | tf_op jit(solution)/shard_map/pallas_call | solution.py:376

commit v5 on v4

--- a/solution.py
+++ b/solution.py
@@ -21,7 +21,7 @@
 def kernel(
     nchip, n, grad_ref, weight_ref, q_ref, k_ref, v_ref, seg_ref,
     dq_ref, dk_ref, dv_ref, dw_ref,
-    og, wfull, prob, seg_col, attn, gsum, kv_send, kv_recv,
+    og, wfull, prob, score_grad, seg_col, attn, gsum, kv_send, kv_recv,
     xsend, xrecv, part, rs_send, rs_recv,
     fill_sem, wfill_sem, rsend_sem, rrecv_sem, lsend_sem, lrecv_sem,
     wsend_sem, wrecv_sem, wxsend_sem, wxrecv_sem,
@@ -108,9 +108,9 @@
             rs_send.at[p], rs_recv.at[p], rss_sem.at[p], rsr_sem.at[p],
             device_id=(behind(p) * 2 + core, t), device_id_type=MESH)
 
-    def kv_copy():
-        return pltpu.make_async_remote_copy(
-            kv_send, kv_recv, kvs_sem, kvr_sem, device_id=partner, device_id_type=MESH)
+    def kv_copy(which):
+        return pltpu.make_async_remote_copy(
+            kv_send.at[which], kv_recv.at[which], kvs_sem.at[which], kvr_sem.at[which], device_id=partner, device_id_type=MESH)
 
     def send_own(p):
         @pl.when(has_right)
@@ -255,34 +255,47 @@
 
     lax.fori_loop(0, 2 * nchip + n - 2, step, 0)
 
-    dk_sum = jnp.zeros((length, HD), F32)
-    dv_sum = jnp.zeros((length, HD), F32)
-
-    def backward(b, carry):
-        dk_sum, dv_sum = carry
+    def backward_values(b, dv_sum):
+        at = row_block(b)
+        for h in range(heads):
+            gh = gsum[at, h * HD:(h + 1) * HD].astype(BF16)
+            dv_sum = dv_sum + dot(prob[h, at, :].astype(BF16), gh, 0, 0)
+        return dv_sum
+
+    def backward_keys(b, dk_sum):
         at = row_block(b)
         for h in range(heads):
             cols = slice(h * HD, (h + 1) * HD)
             gh = gsum[at, cols].astype(BF16)
-            p_full = prob[h, at, :]
             delta = jnp.sum(
                 gh.astype(F32) * attn[at, cols].astype(F32), axis=-1, keepdims=True)
-            dv_sum = dv_sum + dot(p_full.astype(BF16), gh, 0, 0)
-            gs = (p_full * (dot(gh, v_ref[...], 1, 1) - delta) * scale).astype(BF16)
+            gs = (prob[h, at, :] * (dot(gh, v_ref[...], 1, 1) - delta) * scale).astype(BF16)
             dk_sum = dk_sum + dot(gs, q_ref[at, cols], 0, 0)
-            dq_ref[at, cols] = dot(gs, k_ref[...], 1, 0).astype(BF16)
-        return dk_sum, dv_sum
-
-    if blocks == 1:
-        dk_sum, dv_sum = backward(0, (dk_sum, dv_sum))
-    else:
-        dk_sum, dv_sum = lax.fori_loop(0, blocks, backward, (dk_sum, dv_sum))
+            score_grad[h, at, :] = gs
+        return dk_sum
+
+    def backward_queries(b, carry):
+        at = row_block(b)
+        for h in range(heads):
+            dq_ref[at, h * HD:(h + 1) * HD] = dot(
+                score_grad[h, at, :], k_ref[...], 1, 0).astype(BF16)
+        return carry
+
+    def over_blocks(body, init):
+        return body(0, init) if blocks == 1 else lax.fori_loop(0, blocks, body, init)
+
+    zero = jnp.zeros((length, HD), F32)
+    dv_sum = over_blocks(backward_values, zero)
+    kv_send[1] = dv_sum.astype(BF16)
+    kv_copy(1).start()
+    dk_sum = over_blocks(backward_keys, zero)
     kv_send[0] = dk_sum.astype(BF16)
-    kv_send[1] = dv_sum.astype(BF16)
-    kv_copy().start()
+    kv_copy(0).start()
+    over_blocks(backward_queries, 0)
     last = nchip - 1
     weight_terms(last)
-    kv_copy().wait_recv()
+    kv_copy(1).wait_recv()
+    kv_copy(0).wait_recv()
     dk_ref[...] = (dk_sum + kv_recv[0].astype(F32)).astype(BF16)
     dv_ref[...] = (dv_sum + kv_recv[1].astype(F32)).astype(BF16)
 
@@ -293,7 +306,8 @@
         total = total + rs_recv[p].astype(F32)
     dw_ref[...] = total * (1.0 / (2 * nchip))
 
-    kv_copy().wait_send()
+    kv_copy(1).wait_send()
+    kv_copy(0).wait_send()
 
     def drain(p, carry):
         x_copy(p).wait_send()
@@ -351,6 +365,7 @@
             pltpu.VMEM((nchip, 2, n, rows, depth), BF16),
             pltpu.VMEM((nchip, 2, depth, width), BF16),
             pltpu.VMEM((heads, length, length), F32),
+            pltpu.VMEM((heads, length, length), BF16),
             pltpu.VMEM((length, 128), jnp.int32),
             pltpu.VMEM((length, width), BF16),
             pltpu.VMEM((length, width), F32),
@@ -366,7 +381,7 @@
             dma((2 * nchip, n - 1)), dma((2 * nchip, n - 1)),
             dma((most,)), dma((most,)), dma((nchip,)), dma((nchip,)),
             dma((nchip,)), dma((nchip,)), dma((most,)), dma((most,)),
-            dma, dma,
+            dma((2,)), dma((2,)),
         ],
         compiler_params=pltpu.CompilerParams(
             collective_id=0, has_side_effects=True, vmem_limit_bytes=56 << 20),

time: 52 us -> 52 us (level)
  no operation moved by 1% of the time
where the time goes in v5:
time: 52 us; the launch traced here: 51.8 us
  Pallas kernels  51.2 us (98%)
  between operations  0.64 us (1%)
    pallas_call x1, Pallas kernels, local(): pl.pallas_call(functools.partial(kernel, nchip, n), out_shape=(jax.ShapeD...  49.1 us
    pallas_call x1, Pallas kernels, local(): pl.pallas_call(hand_out, out_shape=tuple((jax.ShapeDtypeStruct(r.shape, r...  2.06 us

profile of v5, /device:TPU:0, one launch (start us, length us, event | category | flops | bytes accessed | tf_op | source)
XLA Modules:
  0.0 51.8 jit_solution(14774063031100517038)
XLA Ops:
  0.6 49.1 %shard_map.93 = (bf16[256,256]{1,0:T(8,128)(2,1)}, bf16[256,128]{1,0:T(8,128)(2,1)}, bf16[256,128]{1,0:T(8,128)(2,1)}, f32[512,256]{1,0:T(8,128)}) custom-call(bf16[64,4096]{1,0:T(8,128)(2,1)} %bitcast.7, bf16[512,256]{1,0:T(8,128)(2,1)} %weight_ref.1, bf16[256,256]{1,0:T(8,128)(2,1)} %bitcast.8, bf16[256,128]{1,0:T(8,128)(2,1)} %bitcast.10, ...), custom_call_target="tpu_custom_call" | custom-call | flops 1073741824 | bytes 8388608 | tf_op jit(solution)/shard_map/pallas_call | solution.py:354
  49.8 2.1 %shard_map.94 = (bf16[256,256]{1,0:T(8,128)(2,1)}, bf16[256,128]{1,0:T(8,128)(2,1)}, bf16[256,128]{1,0:T(8,128)(2,1)}, f32[512,256]{1,0:T(8,128)}) custom-call(bf16[256,256]{1,0:T(8,128)(2,1)} %get-tuple-element.12.refs_0_, bf16[256,128]{1,0:T(8,128)(2,1)} %get-tuple-element.13.refs_1_, bf16[256,128]{1,0:T(8,128)(2,1)} %get-tuple-element.14.refs_2_, ...), custom_call_target="tpu_custom_call" | custom-call | tf_op jit(solution)/shard_map/pallas_call | solution.py:391
